TPU v7x, 128 devices: a whole 4x4x4 slice. The times are simulated.
128 devices in a mesh: grp: 16 (over z, x_lo, core), col: 8 (over x_hi, y).
Axes of the slice: x: 4 (x_hi: 2, x_lo: 2; x = x_hi * 2 + x_lo), y: 4, z: 4, core: 2. Of those that a mesh axis runs over, the one named last changes fastest.
Arguments:
- constraint_rows: float32 [4096, 16384], P('grp', 'col'), may hold values from -0.125 to 0.125
- shift: float32 [16384], P('col'), may hold values from 0.3 to 1
- group_rows: int32 [16], replicated, may hold values from 1 to 256, 2048 in all
- panel_index: int32 [1], replicated, may hold values from 0 to 31
Outputs:
- panel_factor: float32 [16384, 512], P(('col', 'grp'))
Inputs may be any that keep to these rules, and one draw needn't show every extreme that they name: `group_rows`: the values sum to 2048 and the largest equals 256.
All inputs are finite; a program needn't handle non-finite values.
Results may differ from a plain program's by a relative error of at most 0.000076.
Values sent between devices are 32-bit elements; how exact they have to be, the bound alone decides.
A program may use at most 64 MiB of HBM per device.

v0:
```python
import jax
import jax.numpy as jnp
from jax import lax
from jax.sharding import PartitionSpec as P

PANEL = 512


def picked(x, axis, root):
    return lax.dynamic_index_in_dim(lax.all_gather(x, axis), root, 0, keepdims=False)


def cut_along(x, dim, size):
    before, after = (x.shape[:dim], x.shape[dim + 1 :])
    return jnp.moveaxis(x.reshape(*before, size, -1, *after), dim, 0)


def sent_and_summed(x, axis, dim):
    pieces = cut_along(x, dim, lax.axis_size(axis))
    arrived = lax.all_to_all(pieces, axis, split_axis=0, concat_axis=0, tiled=True)
    return arrived.sum(axis=0)


def product(left, right):
    return lax.dot_general(
        left,
        right,
        (((0,), (0,)), ((), ())),
        precision=lax.Precision.HIGHEST,
        preferred_element_type=jnp.float32,
    )


def gram_rows(left, panel_cols):
    return product(left, panel_cols)


def add_shift(values, shift_part, first_row, start):
    row_ids = first_row + jnp.arange(values.shape[0], dtype=jnp.int32)
    col_ids = jnp.arange(values.shape[1], dtype=jnp.int32)
    on_diag = row_ids[:, None] == start + col_ids[None, :]
    return values + jnp.where(on_diag, shift_part[:, None], jnp.zeros_like(values))


def on_device(constraint_rows, shift, group_rows, panel_index):
    width = constraint_rows.shape[1]
    groups = lax.axis_size("grp")
    col_idx = lax.axis_index("col")
    grp_idx = lax.axis_index("grp")
    share = width // groups
    start = panel_index[0] * PANEL
    owner = start // width
    local = start - owner * width
    live_count = lax.dynamic_index_in_dim(group_rows, grp_idx, keepdims=False)
    row_ids = jnp.arange(constraint_rows.shape[0], dtype=jnp.int32)
    masked = jnp.where(
        (row_ids < live_count)[:, None], constraint_rows, jnp.zeros_like(constraint_rows)
    )
    own_cols = lax.dynamic_slice_in_dim(masked, local, PANEL, 1)
    panel_cols = picked(own_cols, "col", owner)
    mine = sent_and_summed(gram_rows(masked, panel_cols), "grp", 0)
    shift_part = lax.dynamic_slice_in_dim(shift, grp_idx * share, share, 0)
    mine = add_shift(mine, shift_part, col_idx * width + grp_idx * share, start)
    from_owner = picked(mine, "col", owner)
    owner_shard = lax.all_gather(from_owner, "grp", axis=0, tiled=True)
    block = lax.dynamic_slice_in_dim(owner_shard, local, PANEL, 0)
    factor = jnp.linalg.cholesky(block)
    return lax.linalg.triangular_solve(factor, mine, left_side=False, lower=True, transpose_a=True)


def solution(mesh):
    placed = (P("grp", "col"), P("col"), P(), P())
    return jax.shard_map(
        on_device, mesh=mesh, in_specs=placed, out_specs=P(("col", "grp"), None), check_vma=False
    )
```

profile of v0, /device:TPU:1, one launch (start us, length us, event | category | flops | bytes accessed | tf_op | source)
XLA Modules:
  0.0 386.7 jit_solution(9339683539107075784)
XLA Ops:
  7.2 1.2 dynamic_slice.21
  9.1 1.9 broadcast_select_fusion
  11.1 0.9 constant_dynamic-slice_fusion.3
  12.0 1.5 fusion.41
  13.5 1.9 copy.12
  15.5 70.8 %all-gather.8.cloned.1.call-done = f32[2048,512]{1,0:T(8,128)} async-done(((f32[256,512]{1,0:T(8,128)}), f32[2048,512]{1,0:T(8,128)}) %all-gather.8.cloned.1.call-update) | async-done | bytes 4194320 | tf_op jit(solution)/shard_map/all_gather | solution.py:10
  86.2 6.0 %fusion.1 = f32[16,128,512]{2,1,0:T(8,128)} fusion(f32[16,128,256]{2,1,0:T(8,128)S(1)} %bitcast.65, f32[8,256,512]{2,1,0:T(8,128)} %bitcast.66, s32[]{:T(128)S(6)} %select_n.47), kind=kOutput, calls=%fused_computation.15 | convolution fusion | flops 3221225472 | bytes 6815748 | tf_op jit(solution)/shard_map/dot_general | solution.py:25
  92.3 5.5 %all-to-all-start = ((f32[16,128,512]{2,1,0:T(8,128)}), f32[16,128,512]{2,1,0:T(8,128)}, u32[]{:S(2)}, u32[]{:S(2)}) async-start(f32[16,128,512]{2,1,0:T(8,128)} %fusion.1), calls=%async_computation | async-start | bytes 8388608 | tf_op jit(solution)/shard_map/all_to_all | solution.py:20
  97.8 0.8 dynamic_slice.24
  98.6 48.9 %all-to-all-done = f32[16,128,512]{2,1,0:T(8,128)} async-done(((f32[16,128,512]{2,1,0:T(8,128)}), f32[16,128,512]{2,1,0:T(8,128)}, u32[]{:S(2)}, u32[]{:S(2)}) %all-to-all-start) | async-done | bytes 4194336 | tf_op jit(solution)/shard_map/all_to_all | solution.py:20
  147.5 2.6 reduce_sum.11
  150.1 0.8 bitcast_add_fusion.1
  151.2 50.8 %all-gather.6.cloned.1.call-done = f32[8,128,512]{2,1,0:T(8,128)} async-done(((f32[1,128,512]{2,1,0:T(8,128)}), f32[8,128,512]{2,1,0:T(8,128)}) %all-gather.6.cloned.1.call-update) | async-done | bytes 2097168 | tf_op jit(solution)/shard_map/all_gather | solution.py:10
  201.9 1.7 constant_dynamic-slice_fusion.2
  203.7 36.2 %all-gather.10.cloned.1.call-done = f32[1,2048,512]{2,1,0:T(8,128)} async-done(((f32[1,128,512]{2,1,0:T(8,128)}), f32[1,2048,512]{2,1,0:T(8,128)}) %all-gather.10.cloned.1.call-update) | async-done | bytes 4194320 | tf_op jit(solution)/shard_map/all_gather | solution.py:65
  239.9 1.3 constant_dynamic-slice_fusion.1
  241.5 1.5 fusion
  243.0 11.7 %cholesky.104 = f32[128,128]{1,0:T(8,128)S(1)} custom-call(f32[128,128]{1,0:T(8,128)S(1)} %cholesky.266), custom_call_target="Cholesky" | custom-call | tf_op jit(solution)/shard_map/jit(cholesky)/cholesky | solution.py:67
  254.9 9.8 %custom-call.30 = f32[1,128,128]{1,2,0:T(8,128)S(1)} custom-call(f32[1,128,128]{2,1,0:T(8,128)S(1)} %get-tuple-element.32), custom_call_target="InvertDiagBlocksLowerTriangular" | custom-call | tf_op jit(solution)/shard_map/jit(cholesky)/cholesky | solution.py:67
  265.4 11.7 %cholesky.217 = f32[128,128]{1,0:T(8,128)S(1)} custom-call(f32[128,128]{1,0:T(8,128)S(1)} %cholesky.270), custom_call_target="Cholesky" | custom-call | tf_op jit(solution)/shard_map/jit(cholesky)/cholesky | solution.py:67
  277.1 10.0 %custom-call.31 = f32[1,128,128]{1,2,0:T(8,128)S(1)} custom-call(f32[1,128,128]{2,1,0:T(8,128)S(1)} %get-tuple-element.29), custom_call_target="InvertDiagBlocksLowerTriangular" | custom-call | tf_op jit(solution)/shard_map/jit(cholesky)/cholesky | solution.py:67
  287.8 11.7 %cholesky.238 = f32[128,128]{1,0:T(8,128)S(1)} custom-call(f32[128,128]{1,0:T(8,128)S(1)} %cholesky.275), custom_call_target="Cholesky" | custom-call | tf_op jit(solution)/shard_map/jit(cholesky)/cholesky | solution.py:67
  300.2 9.8 %custom-call.32 = f32[1,128,128]{1,2,0:T(8,128)S(1)} custom-call(f32[1,128,128]{2,1,0:T(8,128)S(1)} %get-tuple-element.26), custom_call_target="InvertDiagBlocksLowerTriangular" | custom-call | tf_op jit(solution)/shard_map/jit(cholesky)/cholesky | solution.py:67
  310.6 11.7 %cholesky.255 = f32[128,128]{1,0:T(8,128)S(1)} custom-call(f32[128,128]{1,0:T(8,128)S(1)} %convolution_subtract_fusion.5), custom_call_target="Cholesky" | custom-call | tf_op jit(solution)/shard_map/jit(cholesky)/cholesky | solution.py:67
  322.3 0.9 compare_reduce_fusion
  326.6 10.1 %while.1 = (s32[]{:T(128)}, f32[512,512]{1,0:T(8,128)S(1)}, s32[4,2]{0,1:T(2,128)S(1)}, f32[4,128,128]{2,1,0:T(8,128)}, s32[]{:T(128)}) while((s32[]{:T(128)}, f32[512,512]{1,0:T(8,128)S(1)}, s32[4,2]{0,1:T(2,128)S(1)}, f32[4,128,128]{2,1,0:T(8,128)}, s32[]{:T(128)}) %tuple.27), condition=%wide.while_cond, body=%wide.while_body.sunk | while | flops 2 | bytes 132705 | solution.py:68
  327.2 1.9 bitcast_dynamic-update-slice_fusion.2
  329.8 1.9 bitcast_dynamic-update-slice_fusion.2
  332.3 1.9 bitcast_dynamic-update-slice_fusion.2
  334.8 1.9 bitcast_dynamic-update-slice_fusion.2
  336.8 40.1 %custom-call.33 = f32[4,128,128]{1,2,0:T(8,128)S(1)} custom-call(f32[4,128,128]{2,1,0:T(8,128)} %get-tuple-element.12), custom_call_target="InvertDiagBlocksLowerTriangular" | custom-call | tf_op jit(solution)/shard_map/triangular_solve | solution.py:68
  379.3 0.8 copy.11
  (49 shorter events, 9.7 us)
Async XLA Ops:
  6.5 79.7 %all-gather.8.cloned.1.call-start = ((), (), s32[]{:S(2)}) async-start(), calls=%async_computation.2 | async-start | bytes 4718592 | tf_op jit(solution)/shard_map/all_gather | solution.py:10
  9.1 2.9 copy-start
  92.3 55.2 %all-to-all-start = ((f32[16,128,512]{2,1,0:T(8,128)}), f32[16,128,512]{2,1,0:T(8,128)}, u32[]{:S(2)}, u32[]{:S(2)}) async-start(f32[16,128,512]{2,1,0:T(8,128)} %fusion.1), calls=%async_computation | async-start | bytes 8388608 | tf_op jit(solution)/shard_map/all_to_all | solution.py:20
  97.8 104.1 %all-gather.6.cloned.1.call-start = ((), (), s32[]{:S(2)}) async-start(), calls=%async_computation.1 | async-start | bytes 2359296 | tf_op jit(solution)/shard_map/all_gather | solution.py:10
  150.9 89.0 %all-gather.10.cloned.1.call-start = ((), (), s32[]{:S(2)}) async-start(), calls=%async_computation.3 | async-start | bytes 4456448 | tf_op jit(solution)/shard_map/all_gather | solution.py:65
Sparse Core Ops, SparseCore 0:
  12.1 74.0 all-gather.7
  151.1 50.8 all-gather.5
  203.7 36.1 all-gather.9
where the time goes:
time: 387 us
  waiting for transfers between devices  207 us (53%)
  other arithmetic  128 us (33%)
  local copies, waits for them, and re-layouts  19.2 us (5%)
  between operations  16.6 us (4%)
  matrix products  10.2 us (3%)
  starting transfers between devices  5.78 us (1%)
    all_gather x2, waiting for transfers between devices, picked(): lax.all_gather(x, axis)  122 us
    another operation x14, other arithmetic, on_device(): factor = jnp.linalg.cholesky(block)  78.8 us
    all_to_all x1, waiting for transfers between devices, sent_and_summed(): lax.all_to_all(pieces, axis, split_axis=0, concat_axis=0, tiled=True)  48.9 us
    another operation x4, other arithmetic, on_device(): lax.linalg.triangular_solve(factor, mine, left_side=False, lower=True, tr...  40.3 us
    all_gather x1, waiting for transfers between devices, on_device(): owner_shard = lax.all_gather(from_owner, 'grp', axis=0, tiled=True)  36.2 us
    another operation x12, local copies, waits for them, and re-layouts  10.1 us
  transfers between devices with their start and end apart: 4, of which 4 were waited for; matrix products, arithmetic and copies ran while one was open for 1% of the time, Pallas kernels for 0%

commit v1 on v0

--- a/solution.py
+++ b/solution.py
@@ -4,6 +4,13 @@
 from jax.sharding import PartitionSpec as P
 
 PANEL = 512
+
+
+def swapped_in(block, axis, d):
+    count = lax.axis_size(axis)
+    blocks = jnp.stack([block for _ in range(count)])
+    blocks = lax.all_to_all(blocks, axis, split_axis=0, concat_axis=0)
+    return jnp.concatenate(blocks, axis=d)
 
 
 def picked(x, axis, root):
@@ -62,7 +69,7 @@
     shift_part = lax.dynamic_slice_in_dim(shift, grp_idx * share, share, 0)
     mine = add_shift(mine, shift_part, col_idx * width + grp_idx * share, start)
     from_owner = picked(mine, "col", owner)
-    owner_shard = lax.all_gather(from_owner, "grp", axis=0, tiled=True)
+    owner_shard = swapped_in(from_owner, "grp", 0)
     block = lax.dynamic_slice_in_dim(owner_shard, local, PANEL, 0)
     factor = jnp.linalg.cholesky(block)
     return lax.linalg.triangular_solve(factor, mine, left_side=False, lower=True, transpose_a=True)

time: 387 us -> 412 us (1.065)
  waiting for transfers between devices: 207 us -> 220 us
  local copies, waits for them, and re-layouts: 19.2 us -> 24.9 us
  starting transfers between devices: 5.78 us -> 11.1 us
    all_to_all x0 -> x1, waiting for transfers between devices: none -> 49.6 us  [swapped_in(): blocks = lax.all_to_all(blocks, axis, split_axis=0, concat_axis=0)]
    all_gather x1 -> x0, waiting for transfers between devices: 36.2 us -> none  [on_device(): owner_shard = lax.all_gather(from_owner, 'grp', axis=0, tiled=True)]
    all_to_all x0 -> x1, starting transfers between devices: none -> 5.53 us  [swapped_in(): blocks = lax.all_to_all(blocks, axis, split_axis=0, concat_axis=0)]
    another operation x12 -> x13, local copies, waits for them, and re-layouts: 10.1 us -> 13 us
where the time goes in v1:
time: 412 us
  waiting for transfers between devices  220 us (53%)
  other arithmetic  128 us (31%)
  local copies, waits for them, and re-layouts  24.9 us (6%)
  between operations  16.9 us (4%)
  starting transfers between devices  11.1 us (3%)
  matrix products  10.2 us (2%)
    all_gather x2, waiting for transfers between devices, picked(): lax.all_gather(x, axis)  122 us
    another operation x14, other arithmetic, on_device(): factor = jnp.linalg.cholesky(block)  78.8 us
    all_to_all x1, waiting for transfers between devices, swapped_in(): blocks = lax.all_to_all(blocks, axis, split_axis=0, concat_axis=0)  49.6 us
    all_to_all x1, waiting for transfers between devices, sent_and_summed(): lax.all_to_all(pieces, axis, split_axis=0, concat_axis=0, tiled=True)  48.9 us
    another operation x4, other arithmetic, on_device(): lax.linalg.triangular_solve(factor, mine, left_side=False, lower=True, tr...  40.3 us
    another operation x12, local copies, waits for them, and re-layouts  10.6 us
  transfers between devices with their start and end apart: 4, of which 4 were waited for; matrix products, arithmetic and copies ran while one was open for 1% of the time, Pallas kernels for 0%

profile of v1, /device:TPU:1, one launch (start us, length us, event | category | flops | bytes accessed | tf_op | source)
XLA Modules:
  0.0 411.6 jit_solution(11087863877796480209)
XLA Ops:
  7.2 1.2 dynamic_slice.23
  9.1 1.9 broadcast_select_fusion
  11.1 0.9 constant_dynamic-slice_fusion.2
  12.0 1.5 fusion.41
  13.5 1.9 copy.17
  15.5 70.8 %all-gather.6.cloned.1.call-done = f32[2048,512]{1,0:T(8,128)} async-done(((f32[256,512]{1,0:T(8,128)}), f32[2048,512]{1,0:T(8,128)}) %all-gather.6.cloned.1.call-update) | async-done | bytes 4194320 | tf_op jit(solution)/shard_map/all_gather | solution.py:17
  86.2 6.0 %fusion.1 = f32[16,128,512]{2,1,0:T(8,128)} fusion(f32[16,128,256]{2,1,0:T(8,128)S(1)} %bitcast.68, f32[8,256,512]{2,1,0:T(8,128)} %bitcast.69, s32[]{:T(128)S(6)} %select_n.47), kind=kOutput, calls=%fused_computation.16 | convolution fusion | flops 3221225472 | bytes 6815748 | tf_op jit(solution)/shard_map/dot_general | solution.py:32
  92.3 5.5 %all-to-all-start = ((f32[16,128,512]{2,1,0:T(8,128)}), f32[16,128,512]{2,1,0:T(8,128)}, u32[]{:S(2)}, u32[]{:S(2)}) async-start(f32[16,128,512]{2,1,0:T(8,128)} %fusion.1), calls=%async_computation | async-start | bytes 8388608 | tf_op jit(solution)/shard_map/all_to_all | solution.py:27
  98.6 48.9 %all-to-all-done = f32[16,128,512]{2,1,0:T(8,128)} async-done(((f32[16,128,512]{2,1,0:T(8,128)}), f32[16,128,512]{2,1,0:T(8,128)}, u32[]{:S(2)}, u32[]{:S(2)}) %all-to-all-start) | async-done | bytes 4194336 | tf_op jit(solution)/shard_map/all_to_all | solution.py:27
  147.5 2.6 reduce_sum.11
  150.9 51.0 %all-gather.4.cloned.1.call-done = f32[8,128,512]{2,1,0:T(8,128)} async-done(((f32[1,128,512]{2,1,0:T(8,128)}), f32[8,128,512]{2,1,0:T(8,128)}) %all-gather.4.cloned.1.call-update) | async-done | bytes 2097168 | tf_op jit(solution)/shard_map/all_gather | solution.py:17
  201.9 1.0 dynamic-slice_bitcast_fusion
  203.0 2.4 stack.2
  205.4 5.5 %all-to-all-start.1 = ((f32[16,128,512]{1,2,0:T(8,128)}), f32[16,128,512]{1,2,0:T(8,128)}, u32[]{:S(2)}, u32[]{:S(2)}) async-start(f32[16,128,512]{1,2,0:T(8,128)} %stack.2), calls=%async_computation.1 | async-start | bytes 8388608 | tf_op jit(solution)/shard_map/all_to_all | solution.py:12
  211.1 49.6 %all-to-all-done.1 = f32[16,128,512]{1,2,0:T(8,128)} async-done(((f32[16,128,512]{1,2,0:T(8,128)}), f32[16,128,512]{1,2,0:T(8,128)}, u32[]{:S(2)}, u32[]{:S(2)}) %all-to-all-start.1) | async-done | bytes 4194336 | tf_op jit(solution)/shard_map/all_to_all | solution.py:12
  260.6 2.7 copy_bitcast_fusion
  263.4 1.9 copy-done
  265.7 1.5 fusion
  267.2 11.7 %cholesky.104 = f32[128,128]{1,0:T(8,128)S(1)} custom-call(f32[128,128]{1,0:T(8,128)S(1)} %cholesky.266), custom_call_target="Cholesky" | custom-call | tf_op jit(solution)/shard_map/jit(cholesky)/cholesky | solution.py:74
  279.1 9.8 %custom-call.30 = f32[1,128,128]{1,2,0:T(8,128)S(1)} custom-call(f32[1,128,128]{2,1,0:T(8,128)S(1)} %get-tuple-element.32), custom_call_target="InvertDiagBlocksLowerTriangular" | custom-call | tf_op jit(solution)/shard_map/jit(cholesky)/cholesky | solution.py:74
  289.6 11.7 %cholesky.217 = f32[128,128]{1,0:T(8,128)S(1)} custom-call(f32[128,128]{1,0:T(8,128)S(1)} %cholesky.270), custom_call_target="Cholesky" | custom-call | tf_op jit(solution)/shard_map/jit(cholesky)/cholesky | solution.py:74
  301.3 10.0 %custom-call.31 = f32[1,128,128]{1,2,0:T(8,128)S(1)} custom-call(f32[1,128,128]{2,1,0:T(8,128)S(1)} %get-tuple-element.29), custom_call_target="InvertDiagBlocksLowerTriangular" | custom-call | tf_op jit(solution)/shard_map/jit(cholesky)/cholesky | solution.py:74
  312.0 11.7 %cholesky.238 = f32[128,128]{1,0:T(8,128)S(1)} custom-call(f32[128,128]{1,0:T(8,128)S(1)} %cholesky.275), custom_call_target="Cholesky" | custom-call | tf_op jit(solution)/shard_map/jit(cholesky)/cholesky | solution.py:74
  324.4 9.8 %custom-call.32 = f32[1,128,128]{1,2,0:T(8,128)S(1)} custom-call(f32[1,128,128]{2,1,0:T(8,128)S(1)} %get-tuple-element.26), custom_call_target="InvertDiagBlocksLowerTriangular" | custom-call | tf_op jit(solution)/shard_map/jit(cholesky)/cholesky | solution.py:74
  334.8 11.9 %cholesky.255 = f32[128,128]{1,0:T(8,128)S(1)} custom-call(f32[128,128]{1,0:T(8,128)S(1)} %convolution_subtract_fusion.5), custom_call_target="Cholesky" | custom-call | tf_op jit(solution)/shard_map/jit(cholesky)/cholesky | solution.py:74
  350.8 10.6 %while.1 = (s32[]{:T(128)}, f32[512,512]{1,0:T(8,128)S(1)}, s32[4,2]{0,1:T(2,128)S(1)}, f32[4,128,128]{2,1,0:T(8,128)}, s32[]{:T(128)}) while((s32[]{:T(128)}, f32[512,512]{1,0:T(8,128)S(1)}, s32[4,2]{0,1:T(2,128)S(1)}, f32[4,128,128]{2,1,0:T(8,128)}, s32[]{:T(128)}) %tuple.27), condition=%wide.while_cond, body=%wide.while_body.sunk | while | flops 2 | bytes 132705 | solution.py:75
  351.5 2.0 bitcast_dynamic-update-slice_fusion.2
  354.1 2.0 bitcast_dynamic-update-slice_fusion.2
  356.8 2.0 bitcast_dynamic-update-slice_fusion.2
  359.4 2.0 bitcast_dynamic-update-slice_fusion.2
  361.4 40.1 %custom-call.33 = f32[4,128,128]{1,2,0:T(8,128)S(1)} custom-call(f32[4,128,128]{2,1,0:T(8,128)} %get-tuple-element.12), custom_call_target="InvertDiagBlocksLowerTriangular" | custom-call | tf_op jit(solution)/shard_map/triangular_solve | solution.py:75
  403.9 0.8 copy.16
  (53 shorter events, 12.4 us)
Async XLA Ops:
  6.5 79.7 %all-gather.6.cloned.1.call-start = ((), (), s32[]{:S(2)}) async-start(), calls=%async_computation.3 | async-start | bytes 4718592 | tf_op jit(solution)/shard_map/all_gather | solution.py:17
  9.1 2.9 copy-start.1
  92.3 55.2 %all-to-all-start = ((f32[16,128,512]{2,1,0:T(8,128)}), f32[16,128,512]{2,1,0:T(8,128)}, u32[]{:S(2)}, u32[]{:S(2)}) async-start(f32[16,128,512]{2,1,0:T(8,128)} %fusion.1), calls=%async_computation | async-start | bytes 8388608 | tf_op jit(solution)/shard_map/all_to_all | solution.py:27
  97.8 104.1 %all-gather.4.cloned.1.call-start = ((), (), s32[]{:S(2)}) async-start(), calls=%async_computation.2 | async-start | bytes 2359296 | tf_op jit(solution)/shard_map/all_gather | solution.py:17
  205.4 55.2 %all-to-all-start.1 = ((f32[16,128,512]{1,2,0:T(8,128)}), f32[16,128,512]{1,2,0:T(8,128)}, u32[]{:S(2)}, u32[]{:S(2)}) async-start(f32[16,128,512]{1,2,0:T(8,128)} %stack.2), calls=%async_computation.1 | async-start | bytes 8388608 | tf_op jit(solution)/shard_map/all_to_all | solution.py:12
  263.3 1.9 copy-start
Sparse Core Ops, SparseCore 0:
  12.1 74.0 all-gather.5
  151.1 50.8 all-gather.3
